TPU v7x, 512 devices: a whole 4x8x8 slice. The times are simulated.
512 devices in a mesh: mp: 8 (over z_hi, core), feat: 64 (over z_lo, x, y).
Axes of the slice: x: 4, y: 8, z: 8 (z_hi: 4, z_lo: 2; z = z_hi * 2 + z_lo), core: 2. Of those that a mesh axis runs over, the one named last changes fastest.
Arguments:
- residual: bfloat16 [2, 384, 2304], P(None, 'feat', 'mp'), may hold values from -6 to 6
- norm_gain: float32 [2, 2304], P(None, 'mp'), may hold values from 0.1 to 1.9
- gate_weight: bfloat16 [2, 2304, 9216], P(None, 'mp', 'feat'), may hold values from -0.125 to 0.125
- up_weight: bfloat16 [2, 2304, 9216], P(None, 'mp', 'feat'), may hold values from -0.125 to 0.125
- down_weight: bfloat16 [2, 9216, 2304], P(None, 'feat', 'mp'), may hold values from -0.0625 to 0.0625
- encoder: bfloat16 [2, 32768, 2304], P(None, 'feat', 'mp'), may hold values from -0.125 to 0.125
- encoder_bias: float32 [2, 32768], P(None, 'feat'), may hold values from -3 to 3
- decoder: bfloat16 [3, 32768, 2304], P(None, 'feat', 'mp'), may hold values from -0.03125 to 0.03125
Outputs:
- grad_encoder: bfloat16 [2, 32768, 2304], P(None, 'feat', 'mp')
- grad_bias: float32 [2, 32768], P(None, 'feat')
- grad_decoder: bfloat16 [3, 32768, 2304], P(None, 'feat', 'mp')
All inputs are finite; a program needn't handle non-finite values.
Results may differ from a plain program's by a relative error of at most 0.02.
The roundings to bfloat16 on the way count: a program that leaves them out, or rounds other values in their place, can miss the bound.
Values may be sent and summed in bfloat16 or wider, within the bound.
A program may use at most 64 MiB of HBM per device.

v0:
```python
import math
import jax
import jax.numpy as jnp
from jax import lax
from jax.sharding import PartitionSpec as P

D = 2304
sparsity_weight = 0.1


def outer_product(weights_side, errors_side):
    return lax.dot_general(
        weights_side, errors_side, (((0,), (0,)), ((), ())), preferred_element_type=jnp.float32
    )


def body(residual, norm_gain, gate_weight, up_weight, down_weight, encoder, encoder_bias, decoder):
    values = residual.astype(jnp.float32)
    squares = lax.psum(jnp.sum(values * values, axis=2), "mp")
    inverse_rms = lax.rsqrt(squares / D + 1e-06)
    normed_local = (values * inverse_rms[:, :, None] * norm_gain[:, None, :]).astype(jnp.bfloat16)
    normed = lax.all_gather(normed_local, "feat", axis=1, tiled=True)
    tokens = normed.shape[1]
    local_rows = residual.shape[1]
    gate_part = jnp.einsum("ltd,ldh->lth", normed, gate_weight, preferred_element_type=jnp.float32)
    up_part = jnp.einsum("ltd,ldh->lth", normed, up_weight, preferred_element_type=jnp.float32)
    gate_part, up_part = (
        lax.psum(gate_part.astype(jnp.bfloat16), "mp").astype(jnp.float32),
        lax.psum(up_part.astype(jnp.bfloat16), "mp").astype(jnp.float32),
    )
    hidden = (jax.nn.gelu(gate_part, approximate=True) * up_part).astype(jnp.bfloat16)
    preact_part = jnp.einsum("ltd,lfd->tlf", normed, encoder, preferred_element_type=jnp.float32)
    preact = lax.psum(preact_part, "mp")
    active = jnp.maximum(preact + encoder_bias[None], 0.0).astype(jnp.bfloat16)
    features = active.shape[2]
    model_cols = decoder.shape[2]
    joined = jnp.concatenate([decoder[1], decoder[2]], axis=0)
    picked = hidden
    partial_value = jnp.einsum(
        "lth,lhd->tld", picked, down_weight, preferred_element_type=jnp.float32
    )
    target = lax.psum_scatter(
        partial_value.reshape(local_rows * lax.axis_size("feat"), -1),
        "feat",
        scatter_dimension=0,
        tiled=True,
    )
    picked = active
    first_part = jnp.dot(picked[:, 0], decoder[0], preferred_element_type=jnp.float32)
    second = jnp.dot(
        picked.reshape(local_rows * lax.axis_size("feat"), 2 * features),
        joined,
        preferred_element_type=jnp.float32,
    )
    rebuilt = lax.psum_scatter(
        jnp.concatenate([first_part, second], axis=1), "feat", scatter_dimension=0, tiled=True
    )
    errors_local = (rebuilt - target).astype(jnp.bfloat16)
    errors = lax.all_gather(errors_local, "feat", axis=0, tiled=True)
    error_first = errors[:, :model_cols]
    error_second = errors[:, model_cols:]
    first_rows = jnp.concatenate([decoder[0], decoder[1]], axis=1)
    back_first = lax.dot_general(
        errors, first_rows, (((1,), (1,)), ((), ())), preferred_element_type=jnp.float32
    )
    back_second = lax.dot_general(
        error_second, decoder[2], (((1,), (1,)), ((), ())), preferred_element_type=jnp.float32
    )
    back_stack = jnp.stack([back_first, back_second], axis=1)
    loss_scale = 1.0 / math.sqrt(tokens)
    backward = lax.psum(back_stack.astype(jnp.bfloat16), "mp").astype(jnp.float32)
    pre_grad = jnp.where(active > 0, loss_scale * (backward + sparsity_weight), 0.0).astype(
        jnp.bfloat16
    )
    grad_encoder = jnp.einsum(
        "tlf,ltd->lfd", pre_grad, normed, preferred_element_type=jnp.float32
    ).astype(jnp.bfloat16)
    grad_bias = jnp.sum(pre_grad.astype(jnp.float32), axis=0)
    active_first = active[:, 0]
    active_second = active[:, 1]
    grad_decoder = (
        loss_scale
        * jnp.stack(
            [
                outer_product(active_first, error_first),
                outer_product(active_first, error_second),
                outer_product(active_second, error_second),
            ]
        )
    ).astype(jnp.bfloat16)
    return (grad_encoder, grad_bias, grad_decoder)


def solution(mesh):
    return jax.shard_map(
        body,
        mesh=mesh,
        in_specs=(
            P(None, "feat", "mp"),
            P(None, "mp"),
            P(None, "mp", "feat"),
            P(None, "mp", "feat"),
            P(None, "feat", "mp"),
            P(None, "feat", "mp"),
            P(None, "feat"),
            P(None, "feat", "mp"),
        ),
        out_specs=(P(None, "feat", "mp"), P(None, "feat"), P(None, "feat", "mp")),
        check_vma=False,
    )
```

profile of v0, /device:TPU:2, one launch (start us, length us, event | category | flops | bytes accessed | tf_op | source)
XLA Modules:
  0.0 1201.8 jit_solution(16398808763718238161)
XLA Ops:
  7.2 0.9 fusion.34
  8.1 22.7 %psum.35 = f32[2,6]{0,1:T(8,128)S(1)} all-reduce(f32[2,6]{0,1:T(8,128)S(1)} %fusion.34), channel_id=1, replica_groups=mesh['mp'=8,'feat'=64] {'mp'}, use_global_device_ids=true, to_apply=%region_1.0 | all-reduce | flops 12 | bytes 96 | tf_op jit(solution)/shard_map/psum | solution.py:19
  31.6 143.9 %all_gather.6 = bf16[2,384,288]{2,0,1:T(2,128)(2,1)S(1)} all-gather(bf16[2,6,288]{2,0,1:T(2,128)(2,1)S(1)} %fusion.36), channel_id=1, replica_groups=mesh['mp'=8,'feat'=64] {'feat'}, dimensions={1}, use_global_device_ids=true | all-gather | bytes 449280 | tf_op jit(solution)/shard_map/all_gather | solution.py:22
  175.5 2.0 convolution_convert_fusion.3
  177.5 1.0 convolution_convert_fusion.4
  178.6 1.7 convolution_bitcast_fusion
  181.3 81.2 %all-reduce.15.cloned.1.call-done = (bf16[2,384,144]{1,2,0:T(8,128)(2,1)}, bf16[2,384,144]{1,2,0:T(8,128)(2,1)}) async-done(((bf16[2,384,144]{1,2,0:T(8,128)(2,1)}, bf16[2,384,144]{1,2,0:T(8,128)(2,1)}), (bf16[2,384,144]{1,2,0:T(8,128)(2,1)}, bf16[2,384,144]{1,2,0:T(8,128)(2,1)})) %all-reduce.15.cloned.1.call-update) | async-done | bytes 442384 | tf_op jit(solution)/shard_map/psum | solution.py:28
  262.6 2.4 fusion.27
  265.0 84.7 %all-reduce.9.cloned.1.call-done = f32[384,2,512]{2,0,1:T(8,128)} async-done(((f32[384,2,512]{2,0,1:T(8,128)}), f32[384,2,512]{2,0,1:T(8,128)}) %all-reduce.9.cloned.1.call-update) | async-done | bytes 1572880 | tf_op jit(solution)/shard_map/psum | solution.py:33
  349.6 1.6 maximum_convert_fusion
  351.2 1.2 copy.16
  352.7 1.8 fusion.3
  354.5 1.0 pad_maximum_fusion
  355.6 1.3 dynamic-slice
  357.5 590.7 %all-reduce.13.cloned.1.call-done = (f32[384,576]{0,1:T(8,128)}, f32[384,576]{0,1:T(8,128)}) async-done(((f32[384,576]{0,1:T(8,128)}, f32[384,576]{0,1:T(8,128)}), (f32[384,576]{0,1:T(8,128)}, f32[384,576]{0,1:T(8,128)})) %all-reduce.13.cloned.1.call-update) | async-done | bytes 1769488
  948.3 1.5 fusion.33
  949.8 146.5 %all-gather = bf16[64,6,576]{2,1,0:T(8,128)(2,1)S(1)} all-gather(bf16[1,6,576]{2,1,0:T(8,128)(2,1)S(1)} %copy.19), channel_id=1, replica_groups=mesh['mp'=8,'feat'=64] {'feat'}, dimensions={0}, use_global_device_ids=true | all-gather | bytes 449280 | tf_op jit(solution)/shard_map/all_gather | solution.py:59
  1096.6 1.4 fusion.1
  1098.0 1.4 fusion.2
  1099.4 1.0 pad_maximum_fusion.1
  1102.0 1.2 fusion
  1103.2 88.5 %all-reduce.11.cloned.1.call-done = bf16[384,2,512]{2,0,1:T(8,128)(2,1)} async-done(((bf16[384,2,512]{2,0,1:T(8,128)(2,1)}), bf16[384,2,512]{2,0,1:T(8,128)(2,1)}) %all-reduce.11.cloned.1.call-update) | async-done | bytes 786448 | tf_op jit(solution)/shard_map/psum | solution.py:71
  1191.6 2.2 convert_reduce_fusion
  1193.9 1.4 convolution_convert_fusion
  (31 shorter events, 4.2 us)
Async XLA Ops:
  7.2 171.4 %copy-start = (bf16[2,512,288]{1,2,0:T(8,128)(2,1)S(1)}, bf16[2,512,288]{1,2,0:T(8,128)(2,1)}, u32[]{:S(2)}) copy-start(bf16[2,512,288]{1,2,0:T(8,128)(2,1)} %param.13) | copy-start | bytes 1769476
  7.2 170.3 %copy-start.5 = (bf16[2,288,144]{1,2,0:T(8,128)(2,1)S(1)}, bf16[2,288,144]{1,2,0:T(8,128)(2,1)}, u32[]{:S(2)}) copy-start(bf16[2,288,144]{1,2,0:T(8,128)(2,1)} %param.10) | copy-start | bytes 497668
  7.2 255.4 %all-reduce.15.cloned.1.call-start = ((), (), s32[]{:S(2)}) async-start(), calls=%async_computation.3 | async-start | bytes 884736 | tf_op jit(solution)/shard_map/psum | solution.py:28
  178.5 1.9 copy-start.2
  178.5 171.1 %all-reduce.9.cloned.1.call-start = ((), (), s32[]{:S(2)}) async-start(), calls=%async_computation | async-start | bytes 3145728 | tf_op jit(solution)/shard_map/psum | solution.py:33
  180.3 82.2 %copy-start.6 = (bf16[2,144,288]{2,1,0:T(8,128)(2,1)S(1)}, bf16[2,144,288]{2,1,0:T(8,128)(2,1)}, u32[]{:S(2)}) copy-start(bf16[2,144,288]{2,1,0:T(8,128)(2,1)} %param.12) | copy-start | bytes 497668
  180.4 169.2 %copy-start.4 = (f32[2,512]{1,0:T(2,128)S(1)}, f32[2,512]{1,0:T(2,128)}, u32[]{:S(2)}) copy-start(f32[2,512]{1,0:T(2,128)} %param.14) | copy-start | bytes 12292
  180.4 767.9 %all-reduce.13.cloned.1.call-start = ((), (), s32[]{:S(2)}) async-start(), calls=%async_computation.2 | async-start | bytes 3538944
  355.5 836.1 %all-reduce.11.cloned.1.call-start = ((), (), s32[]{:S(2)}) async-start(), calls=%async_computation.1 | async-start | bytes 1572864 | tf_op jit(solution)/shard_map/psum | solution.py:71
  1102.0 89.6 %copy-start.1 = (f32[384,2,512]{2,0,1:T(8,128)S(1)}, f32[384,2,512]{2,0,1:T(8,128)}, u32[]{:S(2)}) copy-start(f32[384,2,512]{2,0,1:T(8,128)} %all-reduce.9.cloned.1.call-done) | copy-start | bytes 4718596
  1191.6 2.2 copy-start.3
Sparse Core Ops, SparseCore 0:
  178.7 83.8 all-reduce.14
  265.8 83.7 all-reduce.8
  355.7 592.5 all-reduce.12
  1100.5 91.0 all-reduce.10
where the time goes:
time: 1200 us
  waiting for transfers between devices  845 us (70%)
  blocking collectives  313 us (26%)
  matrix products  15.1 us (1%)
  between operations  14.5 us (1%)
    unnamed x5, waiting for transfers between devices  591 us
    all_gather x1, blocking collectives, body(): errors = lax.all_gather(errors_local, 'feat', axis=0, tiled=True)  146 us
    all_gather x1, blocking collectives, body(): normed = lax.all_gather(normed_local, 'feat', axis=1, tiled=True)  144 us
    psum x1, waiting for transfers between devices, body(): lax.psum(back_stack.astype(jnp.bfloat16), 'mp').astype(jnp.float32)  88.5 us
    psum x1, waiting for transfers between devices, body(): preact = lax.psum(preact_part, 'mp')  84.7 us
    psum x1, waiting for transfers between devices, body(): lax.psum(gate_part.astype(jnp.bfloat16), 'mp').astype(jnp.float32)  81.2 us
  transfers between devices with their start and end apart: 4, of which 4 were waited for; matrix products, arithmetic and copies ran while one was open for 1% of the time, Pallas kernels for 0%

commit v1 on v0

--- a/solution.py
+++ b/solution.py
@@ -56,7 +56,9 @@
         jnp.concatenate([first_part, second], axis=1), "feat", scatter_dimension=0, tiled=True
     )
     errors_local = (rebuilt - target).astype(jnp.bfloat16)
-    errors = lax.all_gather(errors_local, "feat", axis=0, tiled=True)
+    errors = jnp.concatenate(
+        lax.all_to_all(jnp.stack([errors_local] * lax.axis_size("feat")), "feat", 0, 0), axis=0
+    )
     error_first = errors[:, :model_cols]
     error_second = errors[:, model_cols:]
     first_rows = jnp.concatenate([decoder[0], decoder[1]], axis=1)

time: 1200 us -> 1070 us (0.89)
  blocking collectives: 313 us -> 194 us
  waiting for transfers between devices: 845 us -> 833 us
    all_gather x1 -> x0, blocking collectives: 146 us -> none  [body(): errors = lax.all_gather(errors_local, 'feat', axis=0, tiled=True)]
    all_to_all x0 -> x1, blocking collectives: none -> 27.2 us  [body(): lax.all_to_all(jnp.stack([errors_local] * lax.axis_size('feat')), 'feat',...]
    psum x1, waiting for transfers between devices: 88.5 us -> 75.7 us  [body(): lax.psum(back_stack.astype(jnp.bfloat16), 'mp').astype(jnp.float32)]
where the time goes in v1:
time: 1070 us
  waiting for transfers between devices  833 us (78%)
  blocking collectives  194 us (18%)
  matrix products  15.1 us (1%)
  between operations  14.5 us (1%)
    unnamed x5, waiting for transfers between devices  591 us
    all_gather x1, blocking collectives, body(): normed = lax.all_gather(normed_local, 'feat', axis=1, tiled=True)  144 us
    psum x1, waiting for transfers between devices, body(): preact = lax.psum(preact_part, 'mp')  84.6 us
    psum x1, waiting for transfers between devices, body(): lax.psum(gate_part.astype(jnp.bfloat16), 'mp').astype(jnp.float32)  81.3 us
    psum x1, waiting for transfers between devices, body(): lax.psum(back_stack.astype(jnp.bfloat16), 'mp').astype(jnp.float32)  75.7 us
    all_to_all x1, blocking collectives, body(): lax.all_to_all(jnp.stack([errors_local] * lax.axis_size('feat')), 'feat',...  27.2 us
    psum x1, blocking collectives, body(): squares = lax.psum(jnp.sum(values * values, axis=2), 'mp')  22.7 us
  transfers between devices with their start and end apart: 4, of which 4 were waited for; matrix products, arithmetic and copies ran while one was open for 1% of the time, Pallas kernels for 0%

profile of v1, /device:TPU:2, one launch (start us, length us, event | category | flops | bytes accessed | tf_op | source)
XLA Modules:
  0.0 1070.4 jit_solution(14532897572217216971)
XLA Ops:
  7.2 0.9 fusion.32
  8.1 22.7 %psum.35 = f32[2,6]{0,1:T(8,128)S(1)} all-reduce(f32[2,6]{0,1:T(8,128)S(1)} %fusion.32), channel_id=1, replica_groups=mesh['mp'=8,'feat'=64] {'mp'}, use_global_device_ids=true, to_apply=%region_1.0 | all-reduce | flops 12 | bytes 96 | tf_op jit(solution)/shard_map/psum | solution.py:19
  31.6 143.9 %all_gather.3 = bf16[2,384,288]{2,0,1:T(2,128)(2,1)S(1)} all-gather(bf16[2,6,288]{2,0,1:T(2,128)(2,1)S(1)} %fusion.34), channel_id=1, replica_groups=mesh['mp'=8,'feat'=64] {'feat'}, dimensions={1}, use_global_device_ids=true | all-gather | bytes 449280 | tf_op jit(solution)/shard_map/all_gather | solution.py:22
  175.5 2.0 convolution_convert_fusion.3
  177.5 1.0 convolution_convert_fusion.4
  178.6 1.7 convolution_bitcast_fusion
  181.3 81.3 %all-reduce.15.cloned.1.call-done = (bf16[2,384,144]{1,2,0:T(8,128)(2,1)}, bf16[2,384,144]{1,2,0:T(8,128)(2,1)}) async-done(((bf16[2,384,144]{1,2,0:T(8,128)(2,1)}, bf16[2,384,144]{1,2,0:T(8,128)(2,1)}), (bf16[2,384,144]{1,2,0:T(8,128)(2,1)}, bf16[2,384,144]{1,2,0:T(8,128)(2,1)})) %all-reduce.15.cloned.1.call-update) | async-done | bytes 442384 | tf_op jit(solution)/shard_map/psum | solution.py:28
  262.6 2.4 fusion.26
  265.0 84.6 %all-reduce.9.cloned.1.call-done = f32[384,2,512]{2,0,1:T(8,128)} async-done(((f32[384,2,512]{2,0,1:T(8,128)}), f32[384,2,512]{2,0,1:T(8,128)}) %all-reduce.9.cloned.1.call-update) | async-done | bytes 1572880 | tf_op jit(solution)/shard_map/psum | solution.py:33
  349.6 1.6 maximum_convert_fusion
  351.2 1.2 copy.23
  352.7 1.8 fusion.3
  354.5 1.0 pad_maximum_fusion
  355.6 1.3 dynamic-slice
  357.5 591.1 %all-reduce.13.cloned.1.call-done = (f32[384,576]{0,1:T(8,128)}, f32[384,576]{0,1:T(8,128)}) async-done(((f32[384,576]{0,1:T(8,128)}, f32[384,576]{0,1:T(8,128)}), (f32[384,576]{0,1:T(8,128)}, f32[384,576]{0,1:T(8,128)})) %all-reduce.13.cloned.1.call-update) | async-done | bytes 1769488
  948.6 1.5 constant_dynamic-slice_fusion
  950.4 27.2 %all_to_all.5 = bf16[64,6,576]{2,1,0:T(8,128)(2,1)S(1)} all-to-all(bf16[64,6,576]{2,1,0:T(8,128)(2,1)S(1)} %stack.19), channel_id=1, replica_groups=mesh['mp'=8,'feat'=64] {'feat'}, dimensions={0} | all-to-all | bytes 884736 | tf_op jit(solution)/shard_map/all_to_all | solution.py:60
  978.0 1.4 fusion.1
  979.3 1.4 fusion.2
  980.8 1.0 pad_maximum_fusion.1
  983.4 1.2 fusion
  984.5 75.7 %all-reduce.11.cloned.1.call-done = bf16[384,2,512]{2,0,1:T(8,128)(2,1)} async-done(((bf16[384,2,512]{2,0,1:T(8,128)(2,1)}), bf16[384,2,512]{2,0,1:T(8,128)(2,1)}) %all-reduce.11.cloned.1.call-update) | async-done | bytes 786448 | tf_op jit(solution)/shard_map/psum | solution.py:73
  1060.3 2.2 convert_reduce_fusion
  1062.5 1.4 convolution_convert_fusion
  (34 shorter events, 4.5 us)
Async XLA Ops:
  7.2 171.4 %copy-start = (bf16[2,512,288]{1,2,0:T(8,128)(2,1)S(1)}, bf16[2,512,288]{1,2,0:T(8,128)(2,1)}, u32[]{:S(2)}) copy-start(bf16[2,512,288]{1,2,0:T(8,128)(2,1)} %param.13) | copy-start | bytes 1769476
  7.2 170.3 %copy-start.5 = (bf16[2,288,144]{1,2,0:T(8,128)(2,1)S(1)}, bf16[2,288,144]{1,2,0:T(8,128)(2,1)}, u32[]{:S(2)}) copy-start(bf16[2,288,144]{1,2,0:T(8,128)(2,1)} %param.10) | copy-start | bytes 497668
  7.2 255.4 %all-reduce.15.cloned.1.call-start = ((), (), s32[]{:S(2)}) async-start(), calls=%async_computation.4 | async-start | bytes 884736 | tf_op jit(solution)/shard_map/psum | solution.py:28
  178.5 1.9 copy-start.2
  178.6 171.1 %all-reduce.9.cloned.1.call-start = ((), (), s32[]{:S(2)}) async-start(), calls=%async_computation.1 | async-start | bytes 3145728 | tf_op jit(solution)/shard_map/psum | solution.py:33
  180.3 82.2 %copy-start.6 = (bf16[2,144,288]{2,1,0:T(8,128)(2,1)S(1)}, bf16[2,144,288]{2,1,0:T(8,128)(2,1)}, u32[]{:S(2)}) copy-start(bf16[2,144,288]{2,1,0:T(8,128)(2,1)} %param.12) | copy-start | bytes 497668
  180.4 169.3 %copy-start.4 = (f32[2,512]{1,0:T(2,128)S(1)}, f32[2,512]{1,0:T(2,128)}, u32[]{:S(2)}) copy-start(f32[2,512]{1,0:T(2,128)} %param.14) | copy-start | bytes 12292
  180.4 768.2 %all-reduce.13.cloned.1.call-start = ((), (), s32[]{:S(2)}) async-start(), calls=%async_computation.3 | async-start | bytes 3538944
  355.5 704.7 %all-reduce.11.cloned.1.call-start = ((), (), s32[]{:S(2)}) async-start(), calls=%async_computation.2 | async-start | bytes 1572864 | tf_op jit(solution)/shard_map/psum | solution.py:73
  983.4 76.9 %copy-start.1 = (f32[384,2,512]{2,0,1:T(8,128)S(1)}, f32[384,2,512]{2,0,1:T(8,128)}, u32[]{:S(2)}) copy-start(f32[384,2,512]{2,0,1:T(8,128)} %all-reduce.9.cloned.1.call-done) | copy-start | bytes 4718596
  1060.3 2.2 copy-start.3
Sparse Core Ops, SparseCore 0:
  178.7 83.8 all-reduce.14
  265.8 83.7 all-reduce.8
  355.6 592.9 all-reduce.12
  981.9 78.3 all-reduce.10
